TPU v7x, 128 devices: a whole 4x4x4 slice. The times are simulated.
128 devices in a mesh: dp: 16 (over z_lo, x, core), ctx: 8 (over y, z_hi).
Axes of the slice: x: 4, y: 4, z: 4 (z_hi: 2, z_lo: 2; z = z_hi * 2 + z_lo), core: 2. Of those that a mesh axis runs over, the one named last changes fastest.
Arguments:
- inputs: bfloat16 [32, 1024, 576], P('dp', 'ctx'), may hold values from -6 to 6
- segments: int32 [32, 1024], P('dp', 'ctx'), may hold values from 0 to 2, as said below
- cotangent: bfloat16 [32, 1024, 576], P('dp', 'ctx'), may hold values from -6 to 6
- attention_gain: float32 [1, 576], replicated, may hold values from 0.1 to 1.9
- query_weight: bfloat16 [1, 576, 576], P(None, 'dp', 'ctx'), may hold values from -0.25 to 0.25
- key_weight: bfloat16 [1, 576, 192], P(None, 'dp', 'ctx'), may hold values from -0.25 to 0.25
- value_weight: bfloat16 [1, 576, 192], P(None, 'dp', 'ctx'), may hold values from -0.25 to 0.25
- out_weight: bfloat16 [1, 576, 576], P(None, 'dp', 'ctx'), may hold values from -2 to 2
- swiglu_gain: float32 [1, 576], replicated, may hold values from 0.1 to 1.9
- gate_weight: bfloat16 [1, 576, 1536], P(None, 'dp', 'ctx'), may hold values from -0.25 to 0.25
- up_weight: bfloat16 [1, 576, 1536], P(None, 'dp', 'ctx'), may hold values from -0.25 to 0.25
- down_weight: bfloat16 [1, 1536, 576], P(None, 'dp', 'ctx'), may hold values from -0.3125 to 0.3125
Outputs:
- outputs: bfloat16 [32, 1024, 576], P('dp', 'ctx')
- input_grad: float32 [32, 1024, 576], P('dp', 'ctx')
- attention_gain_grad: float32 [1, 576], replicated
- query_grad: float32 [1, 576, 576], P(None, 'dp', 'ctx')
- key_grad: float32 [1, 576, 192], P(None, 'dp', 'ctx')
- value_grad: float32 [1, 576, 192], P(None, 'dp', 'ctx')
- out_grad: float32 [1, 576, 576], P(None, 'dp', 'ctx')
- swiglu_gain_grad: float32 [1, 576], replicated
- gate_grad: float32 [1, 576, 1536], P(None, 'dp', 'ctx')
- up_grad: float32 [1, 576, 1536], P(None, 'dp', 'ctx')
- down_grad: float32 [1, 1536, 576], P(None, 'dp', 'ctx')
Inputs may be any that keep to these rules, and one draw needn't show every extreme that they name: `segments`: segment numbers never fall along a sequence and rise by one at each new document, from 0; every document has 204 positions or more; of the 2 sequences of each index of dp one is a single document and each other holds three.
All inputs are finite; a program needn't handle non-finite values.
Results may differ from a plain program's by a relative error of at most 0.025.
Values may be sent and summed in bfloat16 or wider, within the bound.
No kernel may reach another device: no remote copies, remote signals or barrier semaphores. Data moves between devices by JAX's collectives and lax.ppermute only.
A program may use at most 128 MiB of HBM per device.

v0:
```python
import jax
import jax.numpy as jnp
from jax import lax
from jax.sharding import PartitionSpec as P

HEADS = 9
KV_HEADS = 3
HEAD_DIM = 64
LAYERS = 1


eps = 1e-05
theta = 10000.0
masked = -1e30


def shortened(x):
    return jax.tree.map(lambda a: a.astype(jnp.bfloat16) if a.dtype == jnp.float32 else a, x)


def matmul(left, right):
    return jnp.dot(left, right, preferred_element_type=jnp.float32)


def matmul_tn(left, right):
    return lax.dot_general(
        left, right, (((0,), (0,)), ((), ())), preferred_element_type=jnp.float32
    )


def matmul_nt(left, right):
    return lax.dot_general(
        left, right, (((1,), (1,)), ((), ())), preferred_element_type=jnp.float32
    )


def rms_scale(hidden, gain):
    return hidden * lax.rsqrt(jnp.mean(hidden * hidden, axis=-1, keepdims=True) + eps) * gain


def rotary_tables(positions):
    half_dim = HEAD_DIM // 2
    inverse_freq = theta ** (-(jnp.arange(half_dim, dtype=jnp.float32) * 2.0) / HEAD_DIM)
    angles = positions.astype(jnp.float32)[:, None] * inverse_freq[None, :]
    cosine = jnp.concatenate([jnp.cos(angles), jnp.cos(angles)], axis=-1)
    sine_table = jnp.concatenate([jnp.sin(angles), jnp.sin(angles)], axis=-1)
    return (cosine, sine_table)


def rotate(values, cosine, sine_table):
    half_dim = values.shape[-1] // 2
    turned = jnp.concatenate([-values[..., half_dim:], values[..., :half_dim]], axis=-1)
    return values * cosine[:, None, :] + turned * sine_table[:, None, :]


def swiglu_inner(gate_pre, up_pre):
    return jax.nn.silu(gate_pre) * up_pre


def to_groups(values):
    row_count = values.shape[0]
    group_size = HEADS // KV_HEADS
    shaped = values.reshape(row_count, KV_HEADS, group_size, HEAD_DIM).transpose(1, 2, 0, 3)
    return shaped.reshape(KV_HEADS, group_size * row_count, HEAD_DIM)


def from_groups(values, row_count):
    group_size = HEADS // KV_HEADS
    shaped = values.reshape(KV_HEADS, group_size, row_count, HEAD_DIM).transpose(2, 0, 1, 3)
    return shaped.reshape(row_count, HEADS * HEAD_DIM)


def allowed_mask(row_seg, row_pos, doc_row, offset, span_rows):
    key_seg = lax.dynamic_slice_in_dim(doc_row, offset, span_rows)
    key_pos = offset + jnp.arange(span_rows, dtype=jnp.int32)
    return (row_seg[:, None] == key_seg[None, :]) & (row_pos[:, None] >= key_pos[None, :])


def group_scores(grouped, key_piece, span_rows):
    shaped = key_piece.reshape(span_rows, KV_HEADS, HEAD_DIM)
    return jnp.einsum(
        "hqd,thd->hqt", grouped, shaped, preferred_element_type=jnp.float32
    ) * HEAD_DIM ** (-0.5)


def gather_weights(
    query_weight, key_weight, value_weight, out_weight, gate_weight, up_weight, down_weight
):
    rows_whole = (
        lax.all_gather(query_weight, "dp", axis=1, tiled=True),
        lax.all_gather(key_weight, "dp", axis=1, tiled=True),
        lax.all_gather(value_weight, "dp", axis=1, tiled=True),
        lax.all_gather(out_weight, "dp", axis=1, tiled=True),
        lax.all_gather(gate_weight, "dp", axis=1, tiled=True),
        lax.all_gather(up_weight, "dp", axis=1, tiled=True),
        lax.all_gather(down_weight, "dp", axis=1, tiled=True),
    )
    return (
        lax.all_gather(rows_whole[0], "ctx", axis=2, tiled=True),
        lax.all_gather(rows_whole[1], "ctx", axis=2, tiled=True),
        lax.all_gather(rows_whole[2], "ctx", axis=2, tiled=True),
        lax.all_gather(rows_whole[3], "ctx", axis=2, tiled=True),
        lax.all_gather(rows_whole[4], "ctx", axis=2, tiled=True),
        lax.all_gather(rows_whole[5], "ctx", axis=2, tiled=True),
        lax.all_gather(rows_whole[6], "ctx", axis=2, tiled=True),
    )


def attend(query_b, key_b, value_b, row_seg, row_pos, doc_row):
    row_count = query_b.shape[0]
    grouped = to_groups(query_b)
    maxima = jnp.full(grouped.shape[:2], masked, jnp.float32)
    key_piece = lax.all_gather(key_b, "ctx", axis=0, tiled=True)
    value_piece = lax.all_gather(value_b, "ctx", axis=0, tiled=True)
    span_rows = key_piece.shape[0]
    allowed = allowed_mask(row_seg, row_pos, doc_row, jnp.int32(0), span_rows)[None]
    scores = jnp.where(allowed, group_scores(grouped, key_piece, span_rows), masked)
    newest = jnp.maximum(maxima, jnp.max(scores, axis=-1))
    exponent = jnp.where(allowed, jnp.exp(scores - newest[..., None]), 0.0)
    totals = jnp.sum(exponent, axis=-1)
    shaped_values = value_piece.reshape(span_rows, KV_HEADS, HEAD_DIM).astype(jnp.float32)
    weighted = jnp.einsum(
        "hqt,thd->hqd",
        exponent,
        shaped_values,
        precision=lax.Precision.HIGHEST,
        preferred_element_type=jnp.float32,
    )
    maxima, totals, weighted = (newest, totals, weighted)
    return (from_groups(weighted / totals[..., None], row_count), maxima, totals)


def attend_back(
    grad_b, mixed_f, query_b, key_b, value_b, maxima, totals, row_seg, row_pos, doc_row
):
    row_count = query_b.shape[0]
    score_scale = HEAD_DIM ** (-0.5)
    grouped = to_groups(query_b)
    grad_groups = to_groups(grad_b)
    grad_wide = grad_groups.astype(jnp.float32)
    row_delta = jnp.sum(grad_wide * to_groups(mixed_f), axis=-1)
    whole_keys, whole_values = (
        lax.all_gather(shortened(key_b), "ctx", axis=0, tiled=True).astype(key_b.dtype),
        lax.all_gather(shortened(value_b), "ctx", axis=0, tiled=True).astype(value_b.dtype),
    )
    seq_len = whole_keys.shape[0]
    block_len = min(512, seq_len)

    def visit(query_sum, block_index):
        offset = (block_index * block_len).astype(jnp.int32)
        key_piece = lax.dynamic_slice_in_dim(whole_keys, offset, block_len)
        value_piece = lax.dynamic_slice_in_dim(whole_values, offset, block_len).reshape(
            block_len, KV_HEADS, HEAD_DIM
        )
        allowed = allowed_mask(row_seg, row_pos, doc_row, offset, block_len)[None]
        scores = jnp.where(allowed, group_scores(grouped, key_piece, block_len), masked)
        probs = jnp.where(allowed, jnp.exp(scores - maxima[..., None]) / totals[..., None], 0.0)
        prob_grad = jnp.einsum(
            "hqd,thd->hqt", grad_groups, value_piece, preferred_element_type=jnp.float32
        )
        score_grad = (probs * (prob_grad - row_delta[..., None])).astype(jnp.bfloat16)
        shaped_keys = key_piece.reshape(block_len, KV_HEADS, HEAD_DIM)
        query_sum = query_sum + score_scale * jnp.einsum(
            "hqt,thd->hqd", score_grad, shaped_keys, preferred_element_type=jnp.float32
        )
        key_part = score_scale * jnp.einsum(
            "hqt,hqd->thd", score_grad, grouped, preferred_element_type=jnp.float32
        )
        value_part = jnp.einsum(
            "hqt,hqd->thd",
            probs,
            grad_wide,
            precision=lax.Precision.HIGHEST,
            preferred_element_type=jnp.float32,
        )
        return (
            query_sum,
            (
                key_part.reshape(block_len, KV_HEADS * HEAD_DIM),
                value_part.reshape(block_len, KV_HEADS * HEAD_DIM),
            ),
        )

    query_sum, (key_parts, value_parts) = lax.scan(
        visit,
        jnp.zeros(grouped.shape, jnp.float32),
        jnp.arange(seq_len // block_len, dtype=jnp.int32),
    )
    key_all = key_parts.reshape(seq_len, KV_HEADS * HEAD_DIM)
    value_all = value_parts.reshape(seq_len, KV_HEADS * HEAD_DIM)
    key_share, value_share = (
        lax.psum_scatter(
            key_all.astype(jnp.bfloat16), "ctx", scatter_dimension=0, tiled=True
        ).astype(jnp.float32),
        lax.psum_scatter(
            value_all.astype(jnp.bfloat16), "ctx", scatter_dimension=0, tiled=True
        ).astype(jnp.float32),
    )
    return (from_groups(query_sum, row_count), key_share, value_share)


def layer_forward(
    hidden, weights, first_gain, second_gain, cosine, sine_table, row_seg, row_pos, doc_row
):
    query_full, key_full, value_full, out_full, gate_full, up_full, down_full = weights
    row_count = hidden.shape[0]
    normed = rms_scale(hidden, first_gain).astype(jnp.bfloat16)
    query_pre = matmul(normed, query_full)
    key_pre = matmul(normed, key_full)
    value_b = matmul(normed, value_full).astype(jnp.bfloat16)
    query_b = (
        rotate(query_pre.reshape(row_count, HEADS, HEAD_DIM), cosine, sine_table)
        .reshape(row_count, HEADS * HEAD_DIM)
        .astype(jnp.bfloat16)
    )
    key_b = (
        rotate(key_pre.reshape(row_count, KV_HEADS, HEAD_DIM), cosine, sine_table)
        .reshape(row_count, KV_HEADS * HEAD_DIM)
        .astype(jnp.bfloat16)
    )
    mixed_f, maxima, totals = attend(query_b, key_b, value_b, row_seg, row_pos, doc_row)
    mixed_b = mixed_f.astype(jnp.bfloat16)
    middle = hidden + matmul(mixed_b, out_full)
    second = rms_scale(middle, second_gain).astype(jnp.bfloat16)
    gate_pre = matmul(second, gate_full)
    up_pre = matmul(second, up_full)
    inner_b = swiglu_inner(gate_pre, up_pre).astype(jnp.bfloat16)
    result = middle + matmul(inner_b, down_full)
    stored_acts = (
        hidden,
        normed,
        query_b,
        key_b,
        value_b,
        mixed_f,
        mixed_b,
        maxima,
        totals,
        middle,
        second,
        gate_pre,
        up_pre,
        inner_b,
    )
    return (result, stored_acts)


def layer_backward(
    gradient,
    stored_acts,
    weights,
    first_gain,
    second_gain,
    cosine,
    sine_table,
    row_seg,
    row_pos,
    doc_row,
):
    query_full, key_full, value_full, out_full, gate_full, up_full, down_full = weights
    (
        hidden,
        normed,
        query_b,
        key_b,
        value_b,
        mixed_f,
        mixed_b,
        maxima,
        totals,
        middle,
        second,
        gate_pre,
        up_pre,
        inner_b,
    ) = stored_acts
    row_count = hidden.shape[0]
    grad_b = gradient.astype(jnp.bfloat16)
    down_term = matmul_tn(inner_b, grad_b)
    inner_grad = matmul_nt(grad_b, down_full)
    swiglu_pull = jax.vjp(swiglu_inner, gate_pre, up_pre)[1]
    gate_grad, up_grad = swiglu_pull(inner_grad)
    gate_grad_b = gate_grad.astype(jnp.bfloat16)
    up_grad_b = up_grad.astype(jnp.bfloat16)
    gate_term = matmul_tn(second, gate_grad_b)
    up_term = matmul_tn(second, up_grad_b)
    second_grad = matmul_nt(gate_grad_b, gate_full) + matmul_nt(up_grad_b, up_full)
    norm_pull = jax.vjp(rms_scale, middle, second_gain)[1]
    middle_norm_grad, second_gain_term = norm_pull(second_grad)
    middle_grad = gradient + middle_norm_grad
    middle_b = middle_grad.astype(jnp.bfloat16)
    out_term = matmul_tn(mixed_b, middle_b)
    mixed_grad_b = matmul_nt(middle_b, out_full).astype(jnp.bfloat16)
    turned_query, key_share, value_share = attend_back(
        mixed_grad_b, mixed_f, query_b, key_b, value_b, maxima, totals, row_seg, row_pos, doc_row
    )
    query_pull = jax.vjp(
        lambda values: rotate(values, cosine, sine_table),
        jnp.zeros((row_count, HEADS, HEAD_DIM), jnp.float32),
    )[1]
    key_pull = jax.vjp(
        lambda values: rotate(values, cosine, sine_table),
        jnp.zeros((row_count, KV_HEADS, HEAD_DIM), jnp.float32),
    )[1]
    query_pre_b = (
        query_pull(turned_query.reshape(row_count, HEADS, HEAD_DIM))[0]
        .reshape(row_count, HEADS * HEAD_DIM)
        .astype(jnp.bfloat16)
    )
    key_pre_b = (
        key_pull(key_share.reshape(row_count, KV_HEADS, HEAD_DIM))[0]
        .reshape(row_count, KV_HEADS * HEAD_DIM)
        .astype(jnp.bfloat16)
    )
    value_pre_b = value_share.astype(jnp.bfloat16)
    query_term = matmul_tn(normed, query_pre_b)
    key_term = matmul_tn(normed, key_pre_b)
    value_term = matmul_tn(normed, value_pre_b)
    normed_grad = (
        matmul_nt(query_pre_b, query_full)
        + matmul_nt(key_pre_b, key_full)
        + matmul_nt(value_pre_b, value_full)
    )
    first_pull = jax.vjp(rms_scale, hidden, first_gain)[1]
    hidden_norm_grad, first_gain_term = first_pull(normed_grad)
    layer_terms = (query_term, key_term, value_term, out_term, gate_term, up_term, down_term)
    return (middle_grad + hidden_norm_grad, layer_terms, first_gain_term, second_gain_term)


def body(
    inputs,
    segments,
    cotangent,
    attention_gain,
    query_weight,
    key_weight,
    value_weight,
    out_weight,
    swiglu_gain,
    gate_weight,
    up_weight,
    down_weight,
):
    batch_count, row_count, feature_count = inputs.shape
    group_size = HEADS // KV_HEADS
    doc_ids = lax.all_gather(segments, "ctx", axis=1, tiled=True)
    query_pos = lax.axis_index("ctx") * row_count + jnp.arange(row_count, dtype=jnp.int32)
    cosine, sine_table = rotary_tables(query_pos)
    row_pos = jnp.tile(query_pos, group_size)
    shards = (
        query_weight,
        key_weight,
        value_weight,
        out_weight,
        gate_weight,
        up_weight,
        down_weight,
    )
    dp_size = lax.axis_size("dp")
    ctx_size = lax.axis_size("ctx")
    stored = gather_weights(
        query_weight, key_weight, value_weight, out_weight, gate_weight, up_weight, down_weight
    )
    grad_start = tuple(
        (
            jnp.zeros(
                (shard.shape[0], shard.shape[1] * dp_size, shard.shape[2] * ctx_size), jnp.float32
            )
            for shard in shards
        )
    )
    gain_start = (
        jnp.zeros(attention_gain.shape, jnp.float32),
        jnp.zeros(swiglu_gain.shape, jnp.float32),
    )
    out_start = jnp.zeros(inputs.shape, jnp.bfloat16)
    input_start = jnp.zeros(inputs.shape, jnp.float32)

    def one_batch(batch_index, state_now):
        grads, gain_grads, outputs, input_grads = state_now
        query_seg = segments[batch_index]
        doc_row = doc_ids[batch_index]
        row_seg = jnp.tile(query_seg, group_size)
        hidden = inputs[batch_index].astype(jnp.float32)
        layer_index = 0
        layer_weights = tuple((stacked[layer_index] for stacked in stored))
        hidden, stored_acts = layer_forward(
            hidden,
            layer_weights,
            attention_gain[layer_index],
            swiglu_gain[layer_index],
            cosine,
            sine_table,
            row_seg,
            row_pos,
            doc_row,
        )
        savings = [stored_acts]
        outputs = outputs.at[batch_index].set(hidden.astype(jnp.bfloat16))
        gradient = cotangent[batch_index].astype(jnp.float32)
        first_grads, second_grads = gain_grads
        for layer_index in reversed(range(LAYERS)):
            layer_weights = tuple((stacked[layer_index] for stacked in stored))
            gradient, layer_terms, first_term, second_term = layer_backward(
                gradient,
                savings[layer_index],
                layer_weights,
                attention_gain[layer_index],
                swiglu_gain[layer_index],
                cosine,
                sine_table,
                row_seg,
                row_pos,
                doc_row,
            )
            grads = tuple(
                (stacked.at[layer_index].add(term) for stacked, term in zip(grads, layer_terms))
            )
            first_grads = first_grads.at[layer_index].add(first_term)
            second_grads = second_grads.at[layer_index].add(second_term)
        input_grads = input_grads.at[batch_index].set(gradient)
        return (grads, (first_grads, second_grads), outputs, input_grads)

    grads, gain_grads, outputs, input_grads = lax.fori_loop(
        0, batch_count, one_batch, (grad_start, gain_start, out_start, input_start)
    )
    column_share = (
        lax.psum_scatter(
            grads[0].astype(jnp.bfloat16), "ctx", scatter_dimension=2, tiled=True
        ).astype(jnp.float32),
        lax.psum_scatter(
            grads[1].astype(jnp.bfloat16), "ctx", scatter_dimension=2, tiled=True
        ).astype(jnp.float32),
        lax.psum_scatter(
            grads[2].astype(jnp.bfloat16), "ctx", scatter_dimension=2, tiled=True
        ).astype(jnp.float32),
        lax.psum_scatter(
            grads[3].astype(jnp.bfloat16), "ctx", scatter_dimension=2, tiled=True
        ).astype(jnp.float32),
        lax.psum_scatter(
            grads[4].astype(jnp.bfloat16), "ctx", scatter_dimension=2, tiled=True
        ).astype(jnp.float32),
        lax.psum_scatter(
            grads[5].astype(jnp.bfloat16), "ctx", scatter_dimension=2, tiled=True
        ).astype(jnp.float32),
        lax.psum_scatter(
            grads[6].astype(jnp.bfloat16), "ctx", scatter_dimension=2, tiled=True
        ).astype(jnp.float32),
    )
    owned = (
        lax.psum_scatter(
            column_share[0].astype(jnp.bfloat16), "dp", scatter_dimension=1, tiled=True
        ).astype(jnp.float32),
        lax.psum_scatter(
            column_share[1].astype(jnp.bfloat16), "dp", scatter_dimension=1, tiled=True
        ).astype(jnp.float32),
        lax.psum_scatter(
            column_share[2].astype(jnp.bfloat16), "dp", scatter_dimension=1, tiled=True
        ).astype(jnp.float32),
        lax.psum_scatter(
            column_share[3].astype(jnp.bfloat16), "dp", scatter_dimension=1, tiled=True
        ).astype(jnp.float32),
        lax.psum_scatter(
            column_share[4].astype(jnp.bfloat16), "dp", scatter_dimension=1, tiled=True
        ).astype(jnp.float32),
        lax.psum_scatter(
            column_share[5].astype(jnp.bfloat16), "dp", scatter_dimension=1, tiled=True
        ).astype(jnp.float32),
        lax.psum_scatter(
            column_share[6].astype(jnp.bfloat16), "dp", scatter_dimension=1, tiled=True
        ).astype(jnp.float32),
    )
    first_total, second_total = lax.psum((gain_grads[0], gain_grads[1]), ("dp", "ctx"))
    return (
        outputs,
        input_grads,
        first_total,
        owned[0],
        owned[1],
        owned[2],
        owned[3],
        second_total,
        owned[4],
        owned[5],
        owned[6],
    )


def solution(mesh):
    return jax.shard_map(
        body,
        mesh=mesh,
        in_specs=(
            P("dp", "ctx", None),
            P("dp", "ctx"),
            P("dp", "ctx", None),
            P(),
            P(None, "dp", "ctx"),
            P(None, "dp", "ctx"),
            P(None, "dp", "ctx"),
            P(None, "dp", "ctx"),
            P(),
            P(None, "dp", "ctx"),
            P(None, "dp", "ctx"),
            P(None, "dp", "ctx"),
        ),
        out_specs=(
            P("dp", "ctx", None),
            P("dp", "ctx", None),
            P(),
            P(None, "dp", "ctx"),
            P(None, "dp", "ctx"),
            P(None, "dp", "ctx"),
            P(None, "dp", "ctx"),
            P(),
            P(None, "dp", "ctx"),
            P(None, "dp", "ctx"),
            P(None, "dp", "ctx"),
        ),
        check_vma=False,
    )
```

profile of v0, /device:TPU:1, one launch (start us, length us, event | category | flops | bytes accessed | tf_op | source)
XLA Modules:
  0.0 1704.0 jit_solution(15795561935474435318)
XLA Ops:
  8.1 23.5 %all_gather.76 = bf16[1,1536,72]{2,0,1:T(2,128)(2,1)S(1)} all-gather(bf16[1,96,72]{2,0,1:T(2,128)(2,1)S(1)} %copy.137), channel_id=1, replica_groups=mesh['dp'=16,'ctx'=8] {'dp'}, dimensions={1}, use_global_device_ids=true | all-gather | bytes 235008 | tf_op jit(solution)/shard_map/all_gather | solution.py:96
  34.0 18.0 %all_gather.80 = bf16[1,576,192]{2,0,1:T(2,128)(2,1)S(1)} all-gather(bf16[1,36,192]{2,0,1:T(2,128)(2,1)S(1)} %copy.141), channel_id=1, replica_groups=mesh['dp'=16,'ctx'=8] {'dp'}, dimensions={1}, use_global_device_ids=true | all-gather | bytes 235008 | tf_op jit(solution)/shard_map/all_gather | solution.py:95
  53.5 19.3 %all_gather.82 = bf16[1,576,192]{2,0,1:T(2,128)(2,1)S(1)} all-gather(bf16[1,36,192]{2,0,1:T(2,128)(2,1)S(1)} %copy.143), channel_id=1, replica_groups=mesh['dp'=16,'ctx'=8] {'dp'}, dimensions={1}, use_global_device_ids=true | all-gather | bytes 235008 | tf_op jit(solution)/shard_map/all_gather | solution.py:94
  74.4 17.1 %all_gather.78 = bf16[1,576,72]{2,0,1:T(2,128)(2,1)S(1)} all-gather(bf16[1,36,72]{2,0,1:T(2,128)(2,1)S(1)} %copy.139), channel_id=1, replica_groups=mesh['dp'=16,'ctx'=8] {'dp'}, dimensions={1}, use_global_device_ids=true | all-gather | bytes 88128 | tf_op jit(solution)/shard_map/all_gather | solution.py:93
  91.6 32.3 %all_gather.79 = bf16[1,576,576]{1,2,0:T(8,128)(2,1)S(1)} all-gather(bf16[1,576,72]{1,2,0:T(8,128)(2,1)S(1)} %copy.140), channel_id=1, replica_groups=mesh['dp'=16,'ctx'=8] {'ctx'}, dimensions={2}, use_global_device_ids=true | all-gather | bytes 746496 | tf_op jit(solution)/shard_map/all_gather | solution.py:102
  125.2 23.2 %all_gather.74 = bf16[1,576,72]{2,0,1:T(2,128)(2,1)S(1)} all-gather(bf16[1,36,72]{2,0,1:T(2,128)(2,1)S(1)} %copy.135), channel_id=1, replica_groups=mesh['dp'=16,'ctx'=8] {'dp'}, dimensions={1}, use_global_device_ids=true | all-gather | bytes 88128 | tf_op jit(solution)/shard_map/all_gather | solution.py:90
  148.6 17.2 %all_gather.71 = bf16[1,576,24]{2,0,1:T(2,128)(2,1)S(1)} all-gather(bf16[1,36,24]{2,0,1:T(2,128)(2,1)S(1)} %copy.133), channel_id=1, replica_groups=mesh['dp'=16,'ctx'=8] {'dp'}, dimensions={1}, use_global_device_ids=true | all-gather | bytes 29376 | tf_op jit(solution)/shard_map/all_gather | solution.py:92
  165.9 28.7 %all_gather.72 = bf16[1,576,192]{1,2,0:T(8,128)(2,1)S(1)} all-gather(bf16[1,576,24]{1,2,0:T(8,128)(2,1)S(1)} %copy.134), channel_id=1, replica_groups=mesh['dp'=16,'ctx'=8] {'ctx'}, dimensions={2}, use_global_device_ids=true | all-gather | bytes 248832 | tf_op jit(solution)/shard_map/all_gather | solution.py:101
  195.6 24.4 %all_gather.69 = bf16[1,576,24]{2,0,1:T(2,128)(2,1)S(1)} all-gather(bf16[1,36,24]{2,0,1:T(2,128)(2,1)S(1)} %copy.131), channel_id=1, replica_groups=mesh['dp'=16,'ctx'=8] {'dp'}, dimensions={1}, use_global_device_ids=true | all-gather | bytes 29376 | tf_op jit(solution)/shard_map/all_gather | solution.py:91
  220.1 20.4 %all_gather.73 = s32[2,1024]{1,0:T(2,128)} all-gather(s32[2,128]{1,0:T(2,128)} %param.39), channel_id=1, replica_groups=mesh['dp'=16,'ctx'=8] {'ctx'}, dimensions={1}, use_global_device_ids=true | all-gather | bytes 9216 | tf_op jit(solution)/shard_map/all_gather | solution.py:346
  240.5 28.2 %all_gather.70 = bf16[1,576,192]{1,2,0:T(8,128)(2,1)S(1)} all-gather(bf16[1,576,24]{1,2,0:T(8,128)(2,1)S(1)} %copy.132), channel_id=1, replica_groups=mesh['dp'=16,'ctx'=8] {'ctx'}, dimensions={2}, use_global_device_ids=true | all-gather | bytes 248832 | tf_op jit(solution)/shard_map/all_gather | solution.py:100
  270.0 28.9 %all_gather.75 = bf16[1,576,576]{1,2,0:T(8,128)(2,1)S(1)} all-gather(bf16[1,576,72]{1,2,0:T(8,128)(2,1)S(1)} %copy.136), channel_id=1, replica_groups=mesh['dp'=16,'ctx'=8] {'ctx'}, dimensions={2}, use_global_device_ids=true | all-gather | bytes 746496 | tf_op jit(solution)/shard_map/all_gather | solution.py:99
  311.2 532.9 %while.105 = (s32[]{:T(128)}, f32[1,576,576]{2,1,0:T(8,128)}, f32[1,576,192]{1,2,0:T(8,128)}, f32[1,576,192]{1,2,0:T(8,128)}, f32[1,576,576]{2,1,0:T(8,128)}, /*...) while((s32[]{:T(128)}, f32[1,576,576]{2,1,0:T(8,128)}, ...), condition=%wide.region_15.16_spmd.clone, body=%wide.region_0.15_spmd.clone.sunk | while | flops 4567966720 | bytes 206308944 | solution.py:424
  317.3 25.8 %all_gather.88 = bf16[1024,192]{0,1:T(8,128)(2,1)S(1)} all-gather(bf16[128,192]{0,1:T(8,128)(2,1)S(1)} %bitcast.494), channel_id=1, replica_groups=mesh['dp'=16,'ctx'=8] {'ctx'}, dimensions={0}, use_global_device_ids=true | all-gather | bytes 442368 | tf_op jit(solution)/shard_map/while/body/eval_jaxpr/all_gather | solution.py:143
  347.2 26.9 %all_gather.89 = bf16[1024,192]{0,1:T(8,128)(2,1)} all-gather(bf16[128,192]{0,1:T(8,128)(2,1)S(1)} %convolution_convert_fusion.4), channel_id=1, replica_groups=mesh['dp'=16,'ctx'=8] {'ctx'}, dimensions={0}, use_global_device_ids=true | all-gather | bytes 442368 | tf_op jit(solution)/shard_map/while/body/eval_jaxpr/all_gather | solution.py:144
  393.3 18.0 %while.106 = (s32[]{:T(128)}, f32[3,384,64]{1,2,0:T(8,128)S(1)}, bf16[2,512,192]{1,2,0:T(8,128)(2,1)}, bf16[2,512,192]{1,2,0:T(8,128)(2,1)}, s32[2]{0:T(128)S(1)...) while((s32[]{:T(128)}, f32[3,384,64]{1,2,0:T(8,128)S(1)}, ...), condition=%wide.region_8.8_spmd.clone, body=%wide.region_7.7_spmd.clone.sunk | while | flops 760701440 | bytes 21214076 | solution.py:184
  430.7 72.6 %reduce-scatter.33.cloned.1.call-done = bf16[128,192]{1,0:T(8,128)(2,1)} async-done(((bf16[1024,192]{1,0:T(8,128)(2,1)}), bf16[128,192]{1,0:T(8,128)(2,1)}) %reduce-scatter.33.cloned.1.call-update) | async-done | bytes 49168 | tf_op jit(solution)/shard_map/while
  507.7 68.8 %reduce-scatter.35.cloned.1.call-done = bf16[128,192]{1,0:T(8,128)(2,1)} async-done(((bf16[1024,192]{1,0:T(8,128)(2,1)}), bf16[128,192]{1,0:T(8,128)(2,1)}) %reduce-scatter.35.cloned.1.call-update) | async-done | bytes 49168 | tf_op jit(solution)/shard_map/while
  588.8 26.9 %all_gather.88 = bf16[1024,192]{0,1:T(8,128)(2,1)S(1)} all-gather(bf16[128,192]{0,1:T(8,128)(2,1)S(1)} %bitcast.494), channel_id=1, replica_groups=mesh['dp'=16,'ctx'=8] {'ctx'}, dimensions={0}, use_global_device_ids=true | all-gather | bytes 442368 | tf_op jit(solution)/shard_map/while/body/eval_jaxpr/all_gather | solution.py:143
  619.8 27.6 %all_gather.89 = bf16[1024,192]{0,1:T(8,128)(2,1)} all-gather(bf16[128,192]{0,1:T(8,128)(2,1)S(1)} %convolution_convert_fusion.4), channel_id=1, replica_groups=mesh['dp'=16,'ctx'=8] {'ctx'}, dimensions={0}, use_global_device_ids=true | all-gather | bytes 442368 | tf_op jit(solution)/shard_map/while/body/eval_jaxpr/all_gather | solution.py:144
  666.7 18.0 %while.106 = (s32[]{:T(128)}, f32[3,384,64]{1,2,0:T(8,128)S(1)}, bf16[2,512,192]{1,2,0:T(8,128)(2,1)}, bf16[2,512,192]{1,2,0:T(8,128)(2,1)}, s32[2]{0:T(128)S(1)...) while((s32[]{:T(128)}, f32[3,384,64]{1,2,0:T(8,128)S(1)}, ...), condition=%wide.region_8.8_spmd.clone, body=%wide.region_7.7_spmd.clone.sunk | while | flops 760701440 | bytes 21214076 | solution.py:184
  711.9 52.4 %reduce-scatter.33.cloned.1.call-done = bf16[128,192]{1,0:T(8,128)(2,1)} async-done(((bf16[1024,192]{1,0:T(8,128)(2,1)}), bf16[128,192]{1,0:T(8,128)(2,1)}) %reduce-scatter.33.cloned.1.call-update) | async-done | bytes 49168 | tf_op jit(solution)/shard_map/while
  768.7 68.9 %reduce-scatter.35.cloned.1.call-done = bf16[128,192]{1,0:T(8,128)(2,1)} async-done(((bf16[1024,192]{1,0:T(8,128)(2,1)}), bf16[128,192]{1,0:T(8,128)(2,1)}) %reduce-scatter.35.cloned.1.call-update) | async-done | bytes 49168 | tf_op jit(solution)/shard_map/while
  851.1 8.9 copy.154
  861.5 8.8 copy.156
  884.3 38.7 %reduce-scatter.25.cloned.1.call-done = bf16[1,1536,72]{1,2,0:T(8,128)(2,1)} async-done(((bf16[1,1536,576]{1,2,0:T(8,128)(2,1)}), bf16[1,1536,72]{1,2,0:T(8,128)(2,1)}) %reduce-scatter.25.cloned.1.call-update) | async-done | bytes 221200 | tf_op jit(solution)/shard_map/reduce_scatter | solution.py:446
  926.1 434.6 %all-reduce.25.cloned.1.call-done = (bf16[1,576,576]{1,0,2:T(2,128)(2,1)}, bf16[1,576,576]{1,0,2:T(2,128)(2,1)}, bf16[1,576,1536]{1,0,2:T(2,128)(2,1)}, bf16[1,576,1536]{1,0,2:T(2,128)(2,1)}) async-done(((bf16[1,576,576]{1,0,2:T(2,128)(2,1)}, bf16[1,576,576]{1,0,2:T(2,128)(2,1)}, bf16[1,576,1536]{1,0,2:T(2,128)(2,1)}, bf16[1,576,1536]{1,0,2:T(2,128)(2,1)}), (bf16[1,576,576]{1,0,2:T(2,128)(2,1)}, ...) | async-done | bytes 4866064
  1374.0 70.7 %all-reduce.16 = (f32[1,576]{1,0:T(1,128)}, f32[1,576]{1,0:T(1,128)}) all-reduce(f32[1,576]{1,0:T(1,128)S(1)} %copy-done.53, f32[1,576]{1,0:T(1,128)S(1)} %copy-done.56), channel_id=1, replica_groups=mesh['dp'=16,'ctx'=8] {'dp','ctx'}, use_global_device_ids=true, to_apply=%region_16.17 | all-reduce | flops 1152 | bytes 9216 | tf_op jit(solution)/shard_map/psum | solution.py:473
  1444.7 60.1 %reduce-scatter.31.cloned.1.call-done = bf16[1,576,24]{1,2,0:T(8,128)(2,1)} async-done(((bf16[1,576,192]{1,2,0:T(8,128)(2,1)}), bf16[1,576,24]{1,2,0:T(8,128)(2,1)}) %reduce-scatter.31.cloned.1.call-update) | async-done | bytes 27664
  1504.8 51.9 %all-reduce.17 = (bf16[1,576,24]{1,2,0:T(8,128)(2,1)S(1)}, bf16[1,576,24]{1,2,0:T(8,128)(2,1)S(1)}) all-reduce(bf16[1,576,24]{1,2,0:T(8,128)(2,1)} %reduce-scatter.29.cloned.1.call-done, bf16[1,576,24]{1,2,0:T(8,128)(2,1)} %reduce-scatter.31.cloned.1.call-done), channel_id=7, replica_groups=mesh['dp'=16,'ctx'=8] {'dp'}, use_global_device_ids=true, to_apply=%region_20.21.clone | all-reduce | flops 27648 | bytes 110592
  1558.1 6.8 reduce-scatter.27.cloned.1.call-done
  1566.4 125.6 %all-reduce.23.cloned.1.call-done = (bf16[1,576,72]{2,0,1:T(2,128)(2,1)}, bf16[1,576,72]{2,0,1:T(2,128)(2,1)}, bf16[1,576,192]{2,0,1:T(2,128)(2,1)}, bf16[1,576,192]{2,0,1:T(2,128)(2,1)}) async-done(((bf16[1,576,72]{2,0,1:T(2,128)(2,1)}, bf16[1,576,72]{2,0,1:T(2,128)(2,1)}, bf16[1,576,192]{2,0,1:T(2,128)(2,1)}, bf16[1,576,192]{2,0,1:T(2,128)(2,1)}), (bf16[1,576,72]{2,0,1:T(2,128)(2,1)}, ...) | async-done | bytes 608272
  (551 shorter events, 226.1 us)
Async XLA Ops:
  7.2 46.3 %copy-start.58 = (bf16[1,36,192]{2,1,0:T(8,128)(2,1)S(1)}, bf16[1,36,192]{2,1,0:T(8,128)(2,1)}, u32[]{:S(2)}) copy-start(bf16[1,36,192]{2,1,0:T(8,128)(2,1)} %param.47) | copy-start | bytes 41476
  7.2 291.8 %all-gather.4.cloned.1.call-start = ((), (), s32[]{:S(2)}) async-start(), calls=%async_computation.6 | async-start | bytes 1990656 | tf_op jit(solution)/shard_map/all_gather | solution.py:105
  31.6 42.8 %copy-start.63 = (bf16[1,36,72]{2,1,0:T(8,128)(2,1)S(1)}, bf16[1,36,72]{2,1,0:T(8,128)(2,1)}, u32[]{:S(2)}) copy-start(bf16[1,36,72]{2,1,0:T(8,128)(2,1)} %param.45) | copy-start | bytes 15556
  33.2 268.5 %all-gather.6.cloned.1.call-start = ((), (), s32[]{:S(2)}) async-start(), calls=%async_computation.7 | async-start | bytes 2211840 | tf_op jit(solution)/shard_map/all_gather | solution.py:104
  53.4 252.2 %all-gather.8.cloned.1.call-start = ((), (), s32[]{:S(2)}) async-start(), calls=%async_computation.8 | async-start | bytes 2211840 | tf_op jit(solution)/shard_map/all_gather | solution.py:103
  53.5 71.7 %copy-start.64 = (bf16[1,36,72]{2,1,0:T(8,128)(2,1)S(1)}, bf16[1,36,72]{2,1,0:T(8,128)(2,1)}, u32[]{:S(2)}) copy-start(bf16[1,36,72]{2,1,0:T(8,128)(2,1)} %param.42) | copy-start | bytes 15556
  72.9 75.7 %copy-start.65 = (bf16[1,36,24]{1,2,0:T(8,128)(2,1)S(1)}, bf16[1,36,24]{1,2,0:T(8,128)(2,1)}, u32[]{:S(2)}) copy-start(bf16[1,36,24]{1,2,0:T(8,128)(2,1)} %param.44) | copy-start | bytes 5188
  91.5 104.0 %copy-start.66 = (bf16[1,36,24]{1,2,0:T(8,128)(2,1)S(1)}, bf16[1,36,24]{1,2,0:T(8,128)(2,1)}, u32[]{:S(2)}) copy-start(bf16[1,36,24]{1,2,0:T(8,128)(2,1)} %param.43) | copy-start | bytes 5188
  311.2 76.5 %copy-start = (bf16[1,1536,576]{2,1,0:T(8,128)(2,1)}, bf16[1,1536,576]{2,1,0:T(8,128)(2,1)S(1)}, u32[]{:S(2)}) copy-start(bf16[1,1536,576]{2,1,0:T(8,128)(2,1)S(1)} %get-tuple-element.1957) | copy-start | bytes 5308420 | tf_op jit(solution)/shard_map/while
  311.3 192.0 %reduce-scatter.33.cloned.1.call-start = ((), (), s32[]{:S(2)}) async-start(), calls=%async_computation.15 | async-start | bytes 589824 | tf_op jit(solution)/shard_map/while
  346.8 28.9 %copy-start.43 = (f32[3,384]{1,0:T(4,128)}, f32[3,384]{1,0:T(4,128)S(1)}, u32[]{:S(2)}) copy-start(f32[3,384]{1,0:T(4,128)S(1)} %broadcast_maximum_fusion.2) | copy-start | bytes 13828 | tf_op jit(solution)/shard_map/while
  413.4 163.1 %reduce-scatter.35.cloned.1.call-start = ((), (), s32[]{:S(2)}) async-start(), calls=%async_computation.16 | async-start | bytes 589824 | tf_op jit(solution)/shard_map/while
  427.7 77.4 %copy-start.29 = (f32[128,64]{0,1:T(8,128)S(1)}, f32[128,64]{0,1:T(8,128)}, u32[]{:S(2)}) copy-start(f32[128,64]{0,1:T(8,128)} %get-tuple-element.1950) | copy-start | bytes 98308 | tf_op jit(solution)/shard_map/while
  427.7 78.0 %copy-start.21 = (bf16[1,576,192]{1,2,0:T(8,128)(2,1)S(1)}, bf16[1,576,192]{1,2,0:T(8,128)(2,1)}, u32[]{:S(2)}) copy-start(bf16[1,576,192]{1,2,0:T(8,128)(2,1)} %copy-done.20) | copy-start | bytes 663556 | tf_op jit(solution)/shard_map/while
  430.6 150.1 %copy-start.51 = (f32[1,576]{1,0:T(1,128)S(1)}, f32[1,576]{1,0:T(1,128)}, u32[]{:S(2)}) copy-start(f32[1,576]{1,0:T(1,128)} %get-tuple-element.1906) | copy-start | bytes 6916 | tf_op jit(solution)/shard_map/while
  430.6 74.4 %copy-start.55 = (f32[1,576]{1,0:T(1,128)}, f32[1,576]{1,0:T(1,128)S(1)}, u32[]{:S(2)}) copy-start(f32[1,576]{1,0:T(1,128)S(1)} %fusion.310) | copy-start | bytes 6916 | tf_op jit(solution)/shard_map/while
  507.7 75.1 %copy-start.11 = (bf16[1,576,576]{1,2,0:T(8,128)(2,1)S(1)}, bf16[1,576,576]{1,2,0:T(8,128)(2,1)}, u32[]{:S(2)}) copy-start(bf16[1,576,576]{1,2,0:T(8,128)(2,1)} %copy-done.10) | copy-start | bytes 1990660 | tf_op jit(solution)/shard_map/while
  582.8 78.3 %copy-start = (bf16[1,1536,576]{2,1,0:T(8,128)(2,1)}, bf16[1,1536,576]{2,1,0:T(8,128)(2,1)S(1)}, u32[]{:S(2)}) copy-start(bf16[1,1536,576]{2,1,0:T(8,128)(2,1)S(1)} %get-tuple-element.1957) | copy-start | bytes 5308420 | tf_op jit(solution)/shard_map/while
  582.8 181.5 %reduce-scatter.33.cloned.1.call-start = ((), (), s32[]{:S(2)}) async-start(), calls=%async_computation.15 | async-start | bytes 589824 | tf_op jit(solution)/shard_map/while
  619.4 29.7 %copy-start.43 = (f32[3,384]{1,0:T(4,128)}, f32[3,384]{1,0:T(4,128)S(1)}, u32[]{:S(2)}) copy-start(f32[3,384]{1,0:T(4,128)S(1)} %broadcast_maximum_fusion.2) | copy-start | bytes 13828 | tf_op jit(solution)/shard_map/while
  686.7 150.9 %reduce-scatter.35.cloned.1.call-start = ((), (), s32[]{:S(2)}) async-start(), calls=%async_computation.16 | async-start | bytes 589824 | tf_op jit(solution)/shard_map/while
  708.9 57.1 %copy-start.29 = (f32[128,64]{0,1:T(8,128)S(1)}, f32[128,64]{0,1:T(8,128)}, u32[]{:S(2)}) copy-start(f32[128,64]{0,1:T(8,128)} %get-tuple-element.1950) | copy-start | bytes 98308 | tf_op jit(solution)/shard_map/while
  708.9 57.8 %copy-start.21 = (bf16[1,576,192]{1,2,0:T(8,128)(2,1)S(1)}, bf16[1,576,192]{1,2,0:T(8,128)(2,1)}, u32[]{:S(2)}) copy-start(bf16[1,576,192]{1,2,0:T(8,128)(2,1)} %copy-done.20) | copy-start | bytes 663556 | tf_op jit(solution)/shard_map/while
  711.9 130.2 %copy-start.51 = (f32[1,576]{1,0:T(1,128)S(1)}, f32[1,576]{1,0:T(1,128)}, u32[]{:S(2)}) copy-start(f32[1,576]{1,0:T(1,128)} %get-tuple-element.1906) | copy-start | bytes 6916 | tf_op jit(solution)/shard_map/while
  711.9 54.2 %copy-start.55 = (f32[1,576]{1,0:T(1,128)}, f32[1,576]{1,0:T(1,128)S(1)}, u32[]{:S(2)}) copy-start(f32[1,576]{1,0:T(1,128)S(1)} %fusion.310) | copy-start | bytes 6916 | tf_op jit(solution)/shard_map/while
  768.7 75.4 %copy-start.11 = (bf16[1,576,576]{1,2,0:T(8,128)(2,1)S(1)}, bf16[1,576,576]{1,2,0:T(8,128)(2,1)}, u32[]{:S(2)}) copy-start(bf16[1,576,576]{1,2,0:T(8,128)(2,1)} %copy-done.10) | copy-start | bytes 1990660 | tf_op jit(solution)/shard_map/while
  844.2 78.9 %reduce-scatter.25.cloned.1.call-start = ((), (), s32[]{:S(2)}) async-start(), calls=%async_computation.9 | async-start | bytes 1990656 | tf_op jit(solution)/shard_map/reduce_scatter | solution.py:446
  847.6 513.1 %all-reduce.25.cloned.1.call-start = ((), (), s32[]{:S(2)}) async-start(), calls=%async_computation.14 | async-start | bytes 21626880
  879.8 564.9 %reduce-scatter.29.cloned.1.call-start = ((), (), s32[]{:S(2)}) async-start(), calls=%async_computation.11 | async-start | bytes 276480
  881.5 623.3 %reduce-scatter.31.cloned.1.call-start = ((), (), s32[]{:S(2)}) async-start(), calls=%async_computation.12 | async-start | bytes 276480
  882.4 682.5 %reduce-scatter.27.cloned.1.call-start = ((), (), s32[]{:S(2)}) async-start(), calls=%async_computation.10 | async-start | bytes 417792
  926.0 766.0 %all-reduce.23.cloned.1.call-start = ((), (), s32[]{:S(2)}) async-start(), calls=%async_computation.13 | async-start | bytes 3538944
  (114 other events, 296.0 us)
Sparse Core Ops, SparseCore 0:
  33.3 51.7 all-gather.3
  88.0 54.9 all-gather.5
  145.9 54.7 all-gather.7
  413.5 89.7 reduce-scatter.32
  506.7 69.7 reduce-scatter.34
  686.8 77.3 reduce-scatter.32
  767.9 69.6 reduce-scatter.34
  848.8 74.2 reduce-scatter.24
  925.8 434.7 all-reduce.24
  1364.5 70.0 reduce-scatter.28
  1438.3 66.5 reduce-scatter.30
  1507.2 57.6 reduce-scatter.26
  1567.7 124.2 all-reduce.22
where the time goes:
time: 1710 us; the launch traced here: 1700 us
  waiting for transfers between devices  929 us (54%)
  blocking collectives  511 us (30%)
  local copies, waits for them, and re-layouts  106 us (6%)
  matrix products  97.7 us (6%)
  other arithmetic  39.6 us (2%)
    unnamed x14, waiting for transfers between devices  627 us
    while x8, waiting for transfers between devices  263 us
    psum x1, blocking collectives, body(): lax.psum((gain_grads[0], gain_grads[1]), ('dp', 'ctx'))  70.7 us
    all_gather x2, blocking collectives, attend_back(): lax.all_gather(shortened(value_b), 'ctx', axis=0, tiled=True)  54.5 us
    all_gather x2, blocking collectives, attend_back(): lax.all_gather(shortened(key_b), 'ctx', axis=0, tiled=True)  52.7 us
    unnamed x1, blocking collectives  51.9 us
    reduce_scatter x1, waiting for transfers between devices, body(): lax.psum_scatter(grads[6].astype(jnp.bfloat16), 'ctx', scatter_dimension=...  38.7 us
  transfers between devices with their start and end apart: 13, of which 9 were waited for; matrix products, arithmetic and copies ran while one was open for 7% of the time, Pallas kernels for 0%

commit v1 on v0

v1 whole, which is shorter than its diff:
```python
import jax
import jax.numpy as jnp
import numpy as np
from jax import lax
from jax.sharding import PartitionSpec as P

HEADS = 9
KV_HEADS = 3
HEAD_DIM = 64
GROUP = HEADS // KV_HEADS
D = 576
FF = 1536
KV = KV_HEADS * HEAD_DIM

eps = 1e-05
theta = 10000.0
masked = -1e30
bf16 = jnp.bfloat16
f32 = jnp.float32

N_CTX = 8
N_DP = 16
EVERY = ("dp", "ctx")
SAME_CORE = [
    [(zx * 2 + core) * N_CTX + ctx for ctx in range(N_CTX) for zx in range(N_DP // 2)]
    for core in range(2)
]
OTHER_CORE = [(dp * N_CTX + ctx, (dp ^ 1) * N_CTX + ctx) for dp in range(N_DP) for ctx in range(N_CTX)]
WIDTHS = (72, 24, 24, 72, 192, 192)


def matmul(left, right):
    return jnp.dot(left, right, preferred_element_type=f32)


def matmul_tn(left, right):
    return lax.dot_general(left, right, (((0,), (0,)), ((), ())), preferred_element_type=f32)


def matmul_nt(left, right):
    return lax.dot_general(left, right, (((1,), (1,)), ((), ())), preferred_element_type=f32)


def rms_scale(hidden, gain):
    return hidden * lax.rsqrt(jnp.mean(hidden * hidden, axis=-1, keepdims=True) + eps) * gain


def norm_back(x, gain, c):
    rho = lax.rsqrt(jnp.mean(x * x, axis=-1, keepdims=True) + eps)
    w = c * gain
    grad = rho * (w - x * (rho * rho * jnp.mean(w * x, axis=-1, keepdims=True)))
    return grad, jnp.sum(c * x * rho, axis=0, keepdims=True)


def rotary_tables(positions):
    half_dim = HEAD_DIM // 2
    inverse_freq = theta ** (-(jnp.arange(half_dim, dtype=f32) * 2.0) / HEAD_DIM)
    angles = positions.astype(f32)[:, None] * inverse_freq[None, :]
    cosine = jnp.concatenate([jnp.cos(angles), jnp.cos(angles)], axis=-1)
    sine_table = jnp.concatenate([jnp.sin(angles), jnp.sin(angles)], axis=-1)
    return (cosine, sine_table)


def rotate(values, cosine, sine_table):
    rows, width = values.shape
    shaped = values.reshape(rows, width // HEAD_DIM, HEAD_DIM)
    half = HEAD_DIM // 2
    turned = jnp.concatenate([-shaped[..., half:], shaped[..., :half]], axis=-1)
    return (shaped * cosine[:, None, :] + turned * sine_table[:, None, :]).reshape(rows, width)


def rotate_back(values, cosine, sine_table):
    rows, width = values.shape
    shaped = values.reshape(rows, width // HEAD_DIM, HEAD_DIM)
    half = HEAD_DIM // 2
    scaled = shaped * sine_table[:, None, :]
    turned = jnp.concatenate([scaled[..., half:], -scaled[..., :half]], axis=-1)
    return (shaped * cosine[:, None, :] + turned).reshape(rows, width)


def gather_weights(shards):
    core = lax.axis_index("dp") % 2
    down = shards[6][0].reshape(36, 192)
    payload = jnp.concatenate([s[0] for s in shards[:6]] + [down], axis=1)
    slots = jnp.broadcast_to(payload[None], (64, 36, 768))
    mine = lax.all_to_all(slots, EVERY, 0, 0, tiled=True, axis_index_groups=SAME_CORE)
    other = lax.ppermute(mine, EVERY, OTHER_CORE)
    first = jnp.where(core == 0, mine, other)
    second = jnp.where(core == 0, other, mine)
    whole = jnp.stack([first, second]).reshape(2, N_CTX, 8, 36, 768)
    weights = []
    start = 0
    for width in WIDTHS:
        part = whole[..., start : start + width].transpose(2, 0, 3, 1, 4)
        weights.append(part.reshape(D, N_CTX * width))
        start += width
    down = whole[..., D:].reshape(2, N_CTX, 8, 96, 72).transpose(2, 0, 3, 1, 4)
    weights.append(down.reshape(FF, D))
    return weights


def reduce_grads(grads, gains):
    core = lax.axis_index("dp") % 2
    pieces = [
        g.astype(bf16).reshape(8, 2, 36, N_CTX, width).transpose(1, 3, 0, 2, 4)
        for g, width in zip(grads[:6], WIDTHS)
    ]
    down = grads[6].astype(bf16).reshape(8, 2, 96, N_CTX, 72).transpose(1, 3, 0, 2, 4)
    pieces.append(down.reshape(2, N_CTX, 8, 36, 192))
    whole = jnp.concatenate(pieces, axis=-1).reshape(2, 64, 36, 768)
    keep = lax.dynamic_index_in_dim(whole, core, 0, keepdims=False)
    give = lax.dynamic_index_in_dim(whole, 1 - core, 0, keepdims=False)
    got = lax.ppermute(give, EVERY, OTHER_CORE)
    pair = (keep.astype(f32) + got.astype(f32)).astype(bf16)
    high = gains.astype(bf16)
    low = (gains - high.astype(f32)).astype(bf16)
    extra = jnp.concatenate(
        [jnp.pad(p, ((0, 0), (0, 192))) for p in (high, low)], axis=0
    )
    slots = jnp.concatenate([pair, jnp.broadcast_to(extra[None], (64, 4, 768))], axis=1)
    came = lax.all_to_all(slots, EVERY, 0, 0, tiled=True, axis_index_groups=SAME_CORE)
    total = jnp.sum(came.astype(f32), axis=0)
    gain_half = total[36:38, :D] + total[38:40, :D]
    gain_total = gain_half + lax.ppermute(gain_half, EVERY, OTHER_CORE)
    outs = []
    start = 0
    for width in WIDTHS:
        outs.append(total[None, :36, start : start + width])
        start += width
    outs.append(total[:36, D:].reshape(1, 96, 72))
    return outs, gain_total


def body(
    inputs,
    segments,
    cotangent,
    attention_gain,
    query_weight,
    key_weight,
    value_weight,
    out_weight,
    swiglu_gain,
    gate_weight,
    up_weight,
    down_weight,
):
    batch, rows, _ = inputs.shape
    seq = rows * N_CTX
    score_scale = HEAD_DIM ** (-0.5)
    ctx = lax.axis_index("ctx")
    sent = jnp.concatenate([inputs, segments.astype(bf16)[..., None]], axis=-1)
    came = lax.all_gather(sent, "ctx", axis=1, tiled=True)
    wq, wk, wv, wo, wg, wu, wd = gather_weights(
        (query_weight, key_weight, value_weight, out_weight, gate_weight, up_weight, down_weight)
    )
    first_gain = attention_gain[0]
    second_gain = swiglu_gain[0]
    whole = came[..., :D].reshape(batch * seq, D).astype(f32)
    doc = came[..., D].astype(f32)
    hidden = inputs.reshape(batch * rows, D).astype(f32)
    gradient = cotangent.reshape(batch * rows, D).astype(f32)
    grad_b = cotangent.reshape(batch * rows, D)

    query_pos = ctx * rows + jnp.arange(rows, dtype=jnp.int32)
    key_pos = jnp.arange(seq, dtype=jnp.int32)
    allowed = (segments.astype(f32)[:, :, None] == doc[:, None, :]) & (
        query_pos[:, None] >= key_pos[None, :]
    )[None]
    allowed = allowed[:, None, None]
    cos_k, sin_k = rotary_tables(key_pos)
    cos_q, sin_q = rotary_tables(query_pos)
    cos_k, sin_k = jnp.tile(cos_k, (batch, 1)), jnp.tile(sin_k, (batch, 1))
    cos_q, sin_q = jnp.tile(cos_q, (batch, 1)), jnp.tile(sin_q, (batch, 1))

    normed_all = rms_scale(whole, first_gain).astype(bf16)
    normed = rms_scale(hidden, first_gain).astype(bf16)
    keys = rotate(matmul(normed_all, wk), cos_k, sin_k).astype(bf16)
    values = matmul(normed_all, wv).astype(bf16)
    queries = rotate(matmul(normed, wq), cos_q, sin_q).astype(bf16)

    def heads_q(x):
        return x.reshape(batch, rows, KV_HEADS, GROUP, HEAD_DIM).transpose(0, 2, 3, 1, 4)

    def heads_k(x):
        return x.reshape(batch, seq, KV_HEADS, HEAD_DIM).transpose(0, 2, 1, 3)

    def from_q(x):
        return x.transpose(0, 3, 1, 2, 4).reshape(batch * rows, D)

    def from_k(x):
        return x.transpose(0, 2, 1, 3).reshape(batch * seq, KV)

    qh, kh, vh = heads_q(queries), heads_k(keys), heads_k(values)

    def ein(spec, a, b):
        return jnp.einsum(spec, a, b, preferred_element_type=f32)

    scores = jnp.where(allowed, ein("bhgsd,bhtd->bhgst", qh, kh) * score_scale, masked)
    top = jnp.max(scores, axis=-1, keepdims=True)
    expo = jnp.where(allowed, jnp.exp(scores - top), 0.0)
    probs = expo / jnp.sum(expo, axis=-1, keepdims=True)
    probs_b = probs.astype(bf16)
    mixed_h = ein("bhgst,bhtd->bhgsd", probs_b, vh)
    mixed_b = from_q(mixed_h).astype(bf16)
    middle = hidden + matmul(mixed_b, wo)
    second = rms_scale(middle, second_gain).astype(bf16)
    gate = matmul(second, wg)
    up = matmul(second, wu)
    logistic = jax.nn.sigmoid(gate)
    silu = gate * logistic
    inner_b = (silu * up).astype(bf16)
    result = middle + matmul(inner_b, wd)

    down_term = matmul_tn(inner_b, grad_b)
    inner_grad = matmul_nt(grad_b, wd)
    gate_grad_b = (inner_grad * up * (logistic * (1 + gate * (1 - logistic)))).astype(bf16)
    up_grad_b = (inner_grad * silu).astype(bf16)
    gate_term = matmul_tn(second, gate_grad_b)
    up_term = matmul_tn(second, up_grad_b)
    second_grad = matmul_nt(gate_grad_b, wg) + matmul_nt(up_grad_b, wu)
    middle_norm, second_gain_term = norm_back(middle, second_gain, second_grad)
    middle_grad = gradient + middle_norm
    middle_b = middle_grad.astype(bf16)
    out_term = matmul_tn(mixed_b, middle_b)
    mixed_grad = matmul_nt(middle_b, wo).astype(bf16)

    gh = heads_q(mixed_grad)
    prob_grad = ein("bhgsd,bhtd->bhgst", gh, vh)
    delta = jnp.sum(gh.astype(f32) * mixed_h, axis=-1, keepdims=True)
    ds = (probs * (prob_grad - delta)).astype(bf16)
    turned_query = from_q(ein("bhgst,bhtd->bhgsd", ds, kh)) * score_scale
    turned_key = from_k(ein("bhgst,bhgsd->bhtd", ds, qh)) * score_scale
    value_pre = from_k(ein("bhgst,bhgsd->bhtd", probs_b, gh)).astype(bf16)
    query_pre = rotate_back(turned_query, cos_q, sin_q).astype(bf16)
    key_pre = rotate_back(turned_key, cos_k, sin_k).astype(bf16)

    query_term = matmul_tn(normed, query_pre)
    key_term = matmul_tn(normed_all, key_pre)
    value_term = matmul_tn(normed_all, value_pre)

    both = jnp.concatenate([key_pre, value_pre], axis=-1).reshape(batch, N_CTX, rows, 2 * KV)
    both = lax.all_to_all(both.transpose(1, 0, 2, 3), "ctx", 0, 0, tiled=True)
    both = jnp.sum(both.astype(f32), axis=0).reshape(batch * rows, 2 * KV).astype(bf16)
    normed_grad = (
        matmul_nt(query_pre, wq) + matmul_nt(both[:, :KV], wk) + matmul_nt(both[:, KV:], wv)
    )
    hidden_norm, first_gain_term = norm_back(hidden, first_gain, normed_grad)
    input_grad = middle_grad + hidden_norm

    outs, gains = reduce_grads(
        (query_term, key_term, value_term, out_term, gate_term, up_term, down_term),
        jnp.concatenate([first_gain_term, second_gain_term], axis=0),
    )
    return (
        result.astype(bf16).reshape(batch, rows, D),
        input_grad.reshape(batch, rows, D),
        gains[0:1],
        outs[0],
        outs[1],
        outs[2],
        outs[3],
        gains[1:2],
        outs[4],
        outs[5],
        outs[6],
    )


def solution(mesh):
    weight = P(None, "dp", "ctx")
    rows = P("dp", "ctx", None)
    return jax.shard_map(
        body,
        mesh=mesh,
        in_specs=(rows, P("dp", "ctx"), rows, P(), weight, weight, weight, weight, P(), weight, weight, weight),
        out_specs=(rows, rows, P(), weight, weight, weight, weight, P(), weight, weight, weight),
        check_vma=False,
    )
```

time: 1710 us -> 528 us (0.31)
  waiting for transfers between devices: 929 us -> 142 us
  blocking collectives: 511 us -> 0 us
  local copies, waits for them, and re-layouts: 106 us -> 223 us
  matrix products: 97.7 us -> 56.8 us
  starting transfers between devices: 0.51 us -> 31.2 us
    unnamed x14 -> x1, waiting for transfers between devices: 627 us -> 0.02 us
    all_gather x16 -> x0, blocking collectives: 388 us -> none  [the longest x2 54.5 us: attend_back(): lax.all_gather(shortened(value_b), 'ctx', axis=0, tiled=True)]
    while x8 -> x0, waiting for transfers between devices: 263 us -> none
    all_to_all x0 -> x3, waiting for transfers between devices: none -> 117 us  [the longest x1 49.3 us: gather_weights(): lax.all_to_all(slots, EVERY, 0, 0, tiled=True, axis_index_groups=SAME_CORE)]
    reshape x8 -> x26, local copies, waits for them, and re-layouts: 2.86 us -> 99.2 us  [the longest x10 40.7 us: reduce_grads(): g.astype(bf16).reshape(8, 2, 36, N_CTX, width).transpose(1, 3, 0, 2, 4)]
    psum x1 -> x0, blocking collectives: 70.7 us -> none  [body(): lax.psum((gain_grads[0], gain_grads[1]), ('dp', 'ctx'))]
    unnamed x1 -> x0, blocking collectives: 51.9 us -> none
    concatenate x0 -> x7, local copies, waits for them, and re-layouts: none -> 40.3 us  [the longest x5 35.4 us: reduce_grads(): whole = jnp.concatenate(pieces, axis=-1).reshape(2, 64, 36, 768)]
  transfers between devices with their start and end apart: 13 -> 7, of which waited for: 9 -> 4; matrix products, arithmetic and copies ran while one was open for 7% -> 10% of each run, Pallas kernels for 0% -> 0%
where the time goes in v1:
time: 528 us; the launch traced here: 518 us
  local copies, waits for them, and re-layouts  223 us (42%)
  waiting for transfers between devices  142 us (27%)
  matrix products  56.8 us (11%)
  other arithmetic  49.4 us (9%)
  starting transfers between devices  31.2 us (6%)
  between operations  15.5 us (3%)
    all_to_all x1, waiting for transfers between devices, gather_weights(): lax.all_to_all(slots, EVERY, 0, 0, tiled=True, axis_index_groups=SAME_CORE)  49.3 us
    all_to_all x1, waiting for transfers between devices, reduce_grads(): lax.all_to_all(slots, EVERY, 0, 0, tiled=True, axis_index_groups=SAME_CORE)  44.6 us
    reshape x10, local copies, waits for them, and re-layouts, reduce_grads(): g.astype(bf16).reshape(8, 2, 36, N_CTX, width).transpose(1, 3, 0, 2, 4)  40.7 us
    concatenate x5, local copies, waits for them, and re-layouts, reduce_grads(): whole = jnp.concatenate(pieces, axis=-1).reshape(2, 64, 36, 768)  35.4 us
    all_gather x1, waiting for transfers between devices, body(): came = lax.all_gather(sent, 'ctx', axis=1, tiled=True)  25.2 us
    all_to_all x1, waiting for transfers between devices, body(): both = lax.all_to_all(both.transpose(1, 0, 2, 3), 'ctx', 0, 0, tiled=True)  23.3 us
    reshape x6, local copies, waits for them, and re-layouts, gather_weights(): weights.append(part.reshape(D, N_CTX * width))  19.6 us
    unnamed x119, local copies, waits for them, and re-layouts  18 us
  transfers between devices with their start and end apart: 7, of which 4 were waited for; matrix products, arithmetic and copies ran while one was open for 10% of the time, Pallas kernels for 0%

profile of v1, /device:TPU:1, one launch (start us, length us, event | category | flops | bytes accessed | tf_op | source)
XLA Modules:
  0.0 518.1 jit_solution(140974918554996029)
XLA Ops:
  12.8 12.3 %all-to-all-start = ((bf16[64,36,768]{2,1,0:T(8,128)(2,1)}), bf16[64,36,768]{2,1,0:T(8,128)(2,1)}, u32[]{:S(2)}, u32[]{:S(2)}) async-start(bf16[64,36,768]{2,1,0:T(8,128)(2,1)} %broadcast_in_dim.42), calls=%async_computation | async-start | bytes 7864320 | tf_op jit(solution)/shard_map/all_to_all | solution.py:86
  28.7 49.3 %all-to-all-done = bf16[64,36,768]{2,1,0:T(8,128)(2,1)} async-done(((bf16[64,36,768]{2,1,0:T(8,128)(2,1)}), bf16[64,36,768]{2,1,0:T(8,128)(2,1)}, u32[]{:S(2)}, u32[]{:S(2)}) %all-to-all-start) | async-done | bytes 3538976 | tf_op jit(solution)/shard_map/all_to_all | solution.py:86
  78.0 4.8 copy.246
  89.5 25.2 %all-gather.2.cloned.1.call-done = bf16[2,1024,577]{1,2,0:T(8,128)(2,1)} async-done(((bf16[2,128,577]{1,2,0:T(8,128)(2,1)}), bf16[2,1024,577]{1,2,0:T(8,128)(2,1)}) %all-gather.2.cloned.1.call-update) | async-done | bytes 2363408 | tf_op jit(solution)/shard_map/all_gather | solution.py:153
  122.2 7.0 %reshape.423 = bf16[2048,576,1]{0,1,2:T(8,128)(2,1)} reshape(bf16[2,1024,576]{1,0,2:T(2,128)(2,1)} %copy.251) | data formatting | bytes 4718592 | tf_op jit(solution)/shard_map/convert_element_type | solution.py:176
  140.1 4.2 pad_maximum_fusion.1
  170.6 7.1 %reshape.403 = bf16[2,8,8,96,72]{4,3,2,1,0:T(8,128)(2,1)} reshape(bf16[2,8,8,36,192]{4,3,2,1,0:T(8,128)(2,1)} %copy.260) | data formatting | bytes 3538944 | tf_op jit(solution)/shard_map/reshape | solution.py:97
  177.7 6.8 %copy.261 = bf16[8,2,96,8,72]{2,1,0,4,3:T(2,128)(2,1)} copy(bf16[8,2,96,8,72]{4,2,0,3,1:T(8,128)(2,1)} %bitcast.366) | data formatting | bytes 3538944 | tf_op jit(solution)/shard_map/transpose | solution.py:97
  184.5 7.1 %reshape.404 = bf16[1536,576]{0,1:T(8,128)(2,1)S(1)} reshape(bf16[8,2,96,8,72]{2,1,0,4,3:T(2,128)(2,1)} %copy.261) | data formatting | bytes 3538944 | tf_op jit(solution)/shard_map/reshape | solution.py:98
  212.0 4.6 reshape.401
  220.2 4.8 reshape.402
  228.2 8.7 %fusion.98 = (f32[2,3,3,128]{3,2,1,0:T(4,128)S(1)}, f32[2,3,3,128,1024]{4,3,2,1,0:T(8,128)}) fusion(pred[2,128,1024]{2,1,0:T(8,128)(4,1)} %compare_and_fusion, bf16[3,8,2,8,1024]{4,3,2,1,0:T(8,128)(2,1)} %bitcast.392, bf16[2,128,3,3,64]{1,0,4,3,2:T(2,128)(2,1)} %convert_element_type.241), kind=kOutput, calls=%fused_computation.210 | convolution fusion | flops 313787392 | bytes 10789888 | tf_op jit(solution)/shard_map/sub | solution.py:201
  237.0 4.8 fusion.9
  255.7 4.4 bitcast_convert_fusion
  260.2 5.2 multiply_convert_fusion
  302.4 4.2 copy.301
  309.7 8.5 %reshape.417 = bf16[8,2,96,8,72]{2,1,0,4,3:T(2,128)(2,1)} reshape(bf16[1536,576]{0,1:T(8,128)(2,1)} %convolution_convert_fusion) | data formatting | bytes 3538944 | tf_op jit(solution)/shard_map/reshape | solution.py:108
  318.1 6.8 %copy.280 = bf16[8,2,96,8,72]{4,2,0,3,1:T(8,128)(2,1)} copy(bf16[8,2,96,8,72]{2,1,0,4,3:T(2,128)(2,1)} %reshape.417) | data formatting | bytes 3538944 | tf_op jit(solution)/shard_map/reshape | solution.py:108
  325.0 8.3 %concatenate.82 = bf16[2,64,36,192]{3,2,1,0:T(8,128)(2,1)} reshape(bf16[2,8,8,96,72]{4,3,2,1,0:T(8,128)(2,1)} %bitcast.367) | data formatting | bytes 3538944 | tf_op jit(solution)/shard_map/concatenate | solution.py:110
  337.0 4.8 reshape.415
  341.8 5.6 %copy.443 = bf16[8,2,36,8,192]{4,0,3,2,1:T(8,128)(2,1)} copy(bf16[8,2,36,8,192]{4,3,2,1,0:T(8,128)(2,1)} %reshape.415) | data formatting | bytes 3538944 | tf_op jit(solution)/shard_map/reshape | solution.py:105
  347.4 4.6 reshape.416
  351.9 5.8 %copy.442 = bf16[8,2,36,8,192]{4,0,3,2,1:T(8,128)(2,1)} copy(bf16[8,2,36,8,192]{4,3,2,1,0:T(8,128)(2,1)} %reshape.416) | data formatting | bytes 3538944 | tf_op jit(solution)/shard_map/reshape | solution.py:105
  365.8 4.1 copy.300
  369.9 15.1 %concatenate.83 = bf16[2,64,36,768]{3,1,2,0:T(8,128)(2,1)} concatenate(bf16[2,64,36,72]{3,1,2,0:T(8,128)(2,1)} %bitcast.387, bf16[2,64,36,24]{3,1,2,0:T(8,128)(2,1)} %bitcast.389, bf16[2,64,36,24]{3,1,2,0:T(8,128)(2,1)} %bitcast.388, bf16[2,64,36,72]{3,1,2,0:T(8,128)(2,1)} %bitcast.386, bf16[2,64,36,192]{3,1,2,0:T(8,128)(2,1)} %bitcast.368, bf16[2,64,36,192]{3,1,2,0:T(8,128)(2,1)} %bitcast.369, ...), dimensions={3} | concatenate | bytes 14155776 | tf_op jit(solution)/shard_map/concatenate | solution.py:110
  385.0 4.2 dynamic-slice_bitcast_fusion
  397.6 4.4 all-to-all-start.1
  402.1 23.3 %all-to-all-done.1 = bf16[8,2,128,384]{2,1,3,0:T(2,128)(2,1)} async-done(((bf16[8,2,128,384]{2,1,3,0:T(2,128)(2,1)}), bf16[8,2,128,384]{2,1,3,0:T(2,128)(2,1)}, u32[]{:S(2)}, u32[]{:S(2)}) %all-to-all-start.1) | async-done | bytes 1572896 | tf_op jit(solution)/shard_map/all_to_all | solution.py:243
  434.1 4.4 fusion.2
  442.9 6.6 %all-to-all-start.2 = ((bf16[64,40,768]{2,1,0:T(8,128)(2,1)}), bf16[64,40,768]{2,1,0:T(8,128)(2,1)}, u32[]{:S(2)}, u32[]{:S(2)}) async-start(bf16[64,40,768]{2,1,0:T(8,128)(2,1)} %copy.284), calls=%async_computation.2 | async-start | bytes 7864320 | tf_op jit(solution)/shard_map/all_to_all | solution.py:121
  453.2 44.6 %all-to-all-done.2 = bf16[64,40,768]{2,1,0:T(8,128)(2,1)} async-done(((bf16[64,40,768]{2,1,0:T(8,128)(2,1)}), bf16[64,40,768]{2,1,0:T(8,128)(2,1)}, u32[]{:S(2)}, u32[]{:S(2)}) %all-to-all-start.2) | async-done | bytes 3932192 | tf_op jit(solution)/shard_map/all_to_all | solution.py:121
  500.6 4.8 collective-permute-start.2
  (261 shorter events, 186.3 us)
Async XLA Ops:
  7.2 238.4 %copy-start = (bf16[2,128,576]{1,2,0:T(8,128)(2,1)S(1)}, bf16[2,128,576]{1,2,0:T(8,128)(2,1)}, u32[]{:S(2)}) copy-start(bf16[2,128,576]{1,2,0:T(8,128)(2,1)} %param.14) | copy-start | bytes 884740
  12.8 12.4 %copy-start.49 = (s32[2,128]{1,0:T(2,128)S(1)}, s32[2,128]{1,0:T(2,128)}, u32[]{:S(2)}) copy-start(s32[2,128]{1,0:T(2,128)} %param.13) | copy-start | bytes 3076
  12.8 12.4 %copy-start.4 = (bf16[2,128,576]{1,2,0:T(8,128)(2,1)S(1)}, bf16[2,128,576]{1,2,0:T(8,128)(2,1)}, u32[]{:S(2)}) copy-start(bf16[2,128,576]{1,2,0:T(8,128)(2,1)} %param.12) | copy-start | bytes 884740
  12.8 13.2 %copy-start.47 = (f32[1,576]{1,0:T(1,128)S(1)}, f32[1,576]{1,0:T(1,128)}, u32[]{:S(2)}) copy-start(f32[1,576]{1,0:T(1,128)} %param.15) | copy-start | bytes 6916
  12.8 13.3 %copy-start.48 = (f32[1,576]{1,0:T(1,128)S(1)}, f32[1,576]{1,0:T(1,128)}, u32[]{:S(2)}) copy-start(f32[1,576]{1,0:T(1,128)} %param.20) | copy-start | bytes 6916
  12.8 65.2 %all-to-all-start = ((bf16[64,36,768]{2,1,0:T(8,128)(2,1)}), bf16[64,36,768]{2,1,0:T(8,128)(2,1)}, u32[]{:S(2)}, u32[]{:S(2)}) async-start(bf16[64,36,768]{2,1,0:T(8,128)(2,1)} %broadcast_in_dim.42), calls=%async_computation | async-start | bytes 7864320 | tf_op jit(solution)/shard_map/all_to_all | solution.py:86
  25.2 89.5 %all-gather.2.cloned.1.call-start = ((), (), s32[]{:S(2)}) async-start(), calls=%async_computation.3 | async-start | bytes 2691072 | tf_op jit(solution)/shard_map/all_gather | solution.py:153
  82.7 49.7 %collective-permute-start = (bf16[64,36,768]{2,0,1:T(8,128)(2,1)}, bf16[64,36,768]{2,0,1:T(8,128)(2,1)}, u32[]{:S(2)}, u32[]{:S(2)}) collective-permute-start(bf16[64,36,768]{2,0,1:T(8,128)(2,1)} %copy.246), channel_id=1, source_target_pairs={{0,8},{1,9},{2,10},{3,11},{4,12},{5,13},{6,14},{7,15},{8,0},{9,1},... | collective-permute-start | bytes 10616840 | tf_op jit(solution)/shard_map/ppermute | solution.py:87
  85.7 3.8 copy-start.21
  184.5 7.1 %copy-start.38 = (bf16[576,192]{0,1:T(8,128)(2,1)S(1)}, bf16[576,192]{0,1:T(8,128)(2,1)}, u32[]{:S(2)}) copy-start(bf16[576,192]{0,1:T(8,128)(2,1)} %reshape.398) | copy-start | bytes 663556
  204.1 5.0 copy-start.43
  220.2 4.9 copy-start.22
  236.9 4.8 copy-start.26
  247.0 3.3 copy-start.23
  255.7 4.4 copy-start.19
  255.7 4.4 copy-start.32
  255.7 4.5 copy-start.27
  260.2 5.2 %copy-start.25 = (bf16[2048,3,64]{0,2,1:T(8,128)(2,1)S(1)}, bf16[2048,3,64]{0,2,1:T(8,128)(2,1)}, u32[]{:S(2)}) copy-start(bf16[2048,3,64]{0,2,1:T(8,128)(2,1)} %fusion.15) | copy-start | bytes 2359300
  267.0 3.6 copy-start.24
  267.0 3.5 copy-start.29
  282.3 3.8 copy-start.20
  282.4 3.8 copy-start.46
  282.4 3.9 copy-start.45
  291.8 6.0 %copy-start.10 = (bf16[2,72,8,1024]{3,2,0,1:T(8,128)(2,1)S(1)}, bf16[2,72,8,1024]{3,2,0,1:T(8,128)(2,1)}, u32[]{:S(2)}) copy-start(bf16[2,72,8,1024]{3,2,0,1:T(8,128)(2,1)} %copy.319) | copy-start | bytes 7077892
  351.9 5.8 %copy-start.5 = (f32[2,3,8,8,1024]{4,3,0,2,1:T(8,128)S(1)}, f32[2,3,8,8,1024]{4,3,0,2,1:T(8,128)}, u32[]{:S(2)}) copy-start(f32[2,3,8,8,1024]{4,3,0,2,1:T(8,128)} %copy.320) | copy-start | bytes 4718596
  351.9 5.8 %copy-start.41 = (f32[2048,64]{0,1:T(8,128)S(1)}, f32[2048,64]{0,1:T(8,128)}, u32[]{:S(2)}) copy-start(f32[2048,64]{0,1:T(8,128)} %broadcast_multiply_fusion.3) | copy-start | bytes 1572868
  389.2 44.8 %collective-permute-start.1 = (bf16[64,36,768]{2,0,1:T(8,128)(2,1)}, bf16[64,36,768]{2,0,1:T(8,128)(2,1)}, u32[]{:S(2)}, u32[]{:S(2)}) collective-permute-start(bf16[64,36,768]{2,0,1:T(8,128)(2,1)} %dynamic-slice_bitcast_fusion), channel_id=1, source_target_pairs={{0,8},{1,9},{2,10},{3,11},{4,12},{5,13},{6,14},{7,15},{8,0},{9,1},... | collective-permute-start | bytes 10616840 | tf_op jit(solution)/shard_map/ppermute | solution.py:113
  397.6 33.6 %copy-start.36 = (bf16[256,9,64]{0,2,1:T(8,128)(2,1)S(1)}, bf16[256,9,64]{0,2,1:T(8,128)(2,1)}, u32[]{:S(2)}) copy-start(bf16[256,9,64]{0,2,1:T(8,128)(2,1)} %copy-done.35) | copy-start | bytes 884740
  397.6 27.8 %all-to-all-start.1 = ((bf16[8,2,128,384]{2,1,3,0:T(2,128)(2,1)}), bf16[8,2,128,384]{2,1,3,0:T(2,128)(2,1)}, u32[]{:S(2)}, u32[]{:S(2)}) async-start(bf16[8,2,128,384]{2,1,3,0:T(2,128)(2,1)} %copy.271), calls=%async_computation.1 | async-start | bytes 3145728 | tf_op jit(solution)/shard_map/all_to_all | solution.py:243
  402.0 30.7 %copy-start.39 = (bf16[576,192]{0,1:T(8,128)(2,1)S(1)}, bf16[576,192]{0,1:T(8,128)(2,1)}, u32[]{:S(2)}) copy-start(bf16[576,192]{0,1:T(8,128)(2,1)} %reshape.398) | copy-start | bytes 663556
  442.9 54.8 %all-to-all-start.2 = ((bf16[64,40,768]{2,1,0:T(8,128)(2,1)}), bf16[64,40,768]{2,1,0:T(8,128)(2,1)}, u32[]{:S(2)}, u32[]{:S(2)}) async-start(bf16[64,40,768]{2,1,0:T(8,128)(2,1)} %copy.284), calls=%async_computation.2 | async-start | bytes 7864320 | tf_op jit(solution)/shard_map/all_to_all | solution.py:121
  500.6 9.6 %collective-permute-start.2 = (f32[2,576]{1,0:T(2,128)S(1)}, f32[2,576]{1,0:T(2,128)S(1)}, u32[]{:S(2)}, u32[]{:S(2)}) collective-permute-start(f32[2,576]{1,0:T(2,128)S(1)} %slice_add_fusion), channel_id=1, source_target_pairs={{0,8},{1,9},{2,10},{3,11},{4,12},{5,13},{6,14},{7,15},{8,0},{9,1},... | collective-permute-start | bytes 13832 | tf_op jit(solution)/shard_map/ppermute | solution.py:124
  (25 other events, 45.1 us)
Sparse Core Ops, SparseCore 0:
  28.2 86.4 all-gather.1
